TPU v7x, 128 devices: a whole 4x4x4 slice. The times are simulated.
128 devices in a mesh: band: 4 (over x_hi, core), dom: 32 (over z, y, x_lo).
Axes of the slice: x: 4 (x_hi: 2, x_lo: 2; x = x_hi * 2 + x_lo), y: 4, z: 4, core: 2. Of those that a mesh axis runs over, the one named last changes fastest.
Arguments:
- orbitals: float32 [128, 32, 48, 512], P('dom', None, None, 'band'), may hold values from -6 to 6
- potential: float32 [128, 32, 48], P('dom'), may hold values from -1 to 2
- projectors: float32 [256, 4, 4608], P('dom'), may hold values from -0.09375 to 0.09375
- coupling: float32 [256, 4, 4], P('dom'), may hold values from -4 to 4
- atom_plane: int32 [256], P('dom'), may hold values from 0 to 127, as said below
- projector_count: int32 [256], P('dom'), may hold values from 1 to 4
Outputs:
- filtered: float32 [128, 32, 48, 512], P('dom', None, None, 'band')
- gram: float32 [512, 512], replicated
Inputs may be any that keep to these rules, and one draw needn't show every extreme that they name: `atom_plane`: atom a's first plane lies among the 4 planes of dom index a // 8, that is from (a // 8) * 4 to (a // 8) * 4 + 3; the last atom of each dom index starts on that index's last plane.
All inputs are finite; a program needn't handle non-finite values.
Results may differ from a plain program's by a relative error of at most 0.0003.
Values sent between devices are 32-bit elements; how exact they have to be, the bound alone decides.
A program may use at most 192 MiB of HBM per device.

v0:
```python
import jax
import jax.numpy as jnp
from jax import lax
from jax.sharding import PartitionSpec as P

NORB = 512
HALO = 4
SPAN = 3
MAXPROJ = 4
center_weight = -205.0 / 72.0
side_weights = (8.0 / 5.0, -1.0 / 5.0, 8.0 / 315.0, -1.0 / 560.0)
HIGH = lax.Precision.HIGHEST


def with_halo(value, sides, width):
    for axis, dim in sides:
        peers, length = (lax.axis_size(axis), value.shape[dim])
        up = [(i, (i + 1) % peers) for i in range(peers)]
        down = [(j, i) for i, j in up]
        last = lax.slice_in_dim(value, length - width, length, axis=dim)
        first = lax.slice_in_dim(value, 0, width, axis=dim)
        before = lax.ppermute(last, axis, up)
        after = lax.ppermute(first, axis, down)
        value = jnp.concatenate([before, value, after], axis=dim)
    return value


def passed_along(value, axis, steps):
    count = lax.axis_size(axis)
    pairs = [(source, (source + steps) % count) for source in range(count)]
    return lax.ppermute(value, axis, pairs)


def laplacian(orbital_field, padded, planes):
    total = 3.0 * center_weight * orbital_field
    for offset in range(1, 5):
        weight = side_weights[offset - 1]
        total = total + weight * (
            padded[HALO + offset : HALO + offset + planes]
            + padded[HALO - offset : HALO - offset + planes]
        )
        total = total + weight * (
            jnp.roll(orbital_field, offset, 1) + jnp.roll(orbital_field, -offset, 1)
        )
        total = total + weight * (
            jnp.roll(orbital_field, offset, 2) + jnp.roll(orbital_field, -offset, 2)
        )
    return total


def apply_hamiltonian(orbital_field, potential, layout_pieces):
    planes, side_y, side_z, local_orbs = orbital_field.shape
    beta_full, live_mask, sym_coupling = layout_pieces
    padded = with_halo(orbital_field, (("dom", 0),), HALO)
    extended = padded[HALO : HALO + planes + SPAN - 1].reshape(
        planes + SPAN - 1, side_y * side_z, local_orbs
    )
    correlations = (
        jnp.einsum(
            "ajpc,pco->ajo", beta_full, extended, precision=HIGH, preferred_element_type=jnp.float32
        )
        * live_mask[:, :, None]
    )
    weighted = (
        jnp.einsum(
            "aij,ajo->aio",
            sym_coupling,
            correlations,
            precision=HIGH,
            preferred_element_type=jnp.float32,
        )
        * live_mask[:, :, None]
    )
    contrib = jnp.einsum(
        "ajpc,ajo->pco", beta_full, weighted, precision=HIGH, preferred_element_type=jnp.float32
    )
    contrib = contrib.reshape(planes + SPAN - 1, side_y, side_z, local_orbs)
    arrived = passed_along(contrib[planes:], "dom", 1)
    own_planes = contrib[:planes]
    own_planes = jnp.concatenate([own_planes[: SPAN - 1] + arrived, own_planes[SPAN - 1 :]], axis=0)
    kinetic = -0.5 * laplacian(orbital_field, padded, planes)
    return kinetic + potential[:, :, :, None] * orbital_field + own_planes


def shards(orbitals, potential, projectors, coupling, atom_plane, projector_count):
    planes, side_y, side_z, local_orbs = orbitals.shape
    atom_total = projectors.shape[0]
    first_plane = atom_plane - lax.axis_index("dom") * planes
    plane_ids = jnp.arange(planes + SPAN - 1, dtype=jnp.int32)
    span_ids = jnp.arange(SPAN, dtype=jnp.int32)
    onehot = (
        plane_ids[None, None, :] == first_plane[:, None, None] + span_ids[None, :, None]
    ).astype(jnp.float32)
    beta_split = projectors.reshape(atom_total, MAXPROJ, SPAN, side_y * side_z)
    beta_full = jnp.einsum(
        "akp,ajkc->ajpc", onehot, beta_split, precision=HIGH, preferred_element_type=jnp.float32
    )
    slots = jnp.arange(MAXPROJ, dtype=jnp.int32)
    live_mask = (slots[None, :] < projector_count[:, None]).astype(jnp.float32)
    sym_coupling = 0.5 * (coupling + jnp.transpose(coupling, (0, 2, 1)))
    layout_pieces = (beta_full, live_mask, sym_coupling)
    first = (apply_hamiltonian(orbitals, potential, layout_pieces) - 7.0 * orbitals) / 6.0
    second = (
        2.0 * (apply_hamiltonian(first, potential, layout_pieces) - 7.0 * first) / 6.0 - orbitals
    )
    cells = planes * side_y * side_z
    total_cells = cells * lax.axis_size("dom")
    flat = second.reshape(cells, local_orbs)
    identity = jnp.eye(NORB, dtype=jnp.float32)
    panels = lax.all_gather(flat, "band", axis=1, tiled=True)
    partial_gram = jnp.dot(panels.T, panels, precision=HIGH, preferred_element_type=jnp.float32)
    gram = lax.psum(partial_gram, "dom") * (1.0 / total_cells)
    lower = jnp.linalg.cholesky(gram)
    inverse = jax.scipy.linalg.solve_triangular(lower, identity, lower=True)
    own_rows = lax.dynamic_slice_in_dim(inverse, lax.axis_index("band") * local_orbs, local_orbs, 0)
    result = jnp.dot(panels, own_rows.T, precision=HIGH, preferred_element_type=jnp.float32)
    return (result.reshape(planes, side_y, side_z, local_orbs), gram)


def solution(mesh):
    placed = (
        P("dom", None, None, "band"),
        P("dom", None, None),
        P("dom", None, None),
        P("dom", None, None),
        P("dom"),
        P("dom"),
    )
    return jax.shard_map(
        shards,
        mesh=mesh,
        in_specs=placed,
        out_specs=(P("dom", None, None, "band"), P()),
        check_vma=False,
    )
```

profile of v0, /device:TPU:0, one launch (start us, length us, event | category | flops | bytes accessed | tf_op | source)
XLA Modules:
  0.0 1015.1 jit_solution(8115964120412169199)
XLA Ops:
  8.9 6.0 collective-permute-start
  43.0 41.0 %collective-permute-done.1 = f32[4,32,48,128]{3,2,1,0:T(8,128)} collective-permute-done((f32[4,32,48,128]{3,2,1,0:T(8,128)}, f32[4,32,48,128]{3,2,1,0:T(8,128)}, u32[]{:S(2)}, u32[]{:S(2)}) %collective-permute-start.1) | collective-permute-done | bytes 3145760 | tf_op jit(solution)/shard_map/ppermute | solution.py:22
  86.7 59.3 %collective-permute-done = f32[4,32,48,128]{3,2,1,0:T(8,128)} collective-permute-done((f32[4,32,48,128]{3,2,1,0:T(8,128)}, f32[4,32,48,128]{3,2,1,0:T(8,128)}, u32[]{:S(2)}, u32[]{:S(2)}) %collective-permute-start) | collective-permute-done | bytes 3145760 | tf_op jit(solution)/shard_map/ppermute | solution.py:23
  151.8 7.7 convolution_bitcast_fusion.1
  169.7 3.4 fusion.154
  173.1 27.3 %collective-permute-done.2 = f32[2,32,48,128]{3,2,1,0:T(8,128)S(1)} collective-permute-done((f32[2,32,48,128]{3,2,1,0:T(8,128)S(1)}, f32[2,32,48,128]{3,2,1,0:T(8,128)S(1)}, u32[]{:S(2)}, u32[]{:S(2)}) %collective-permute-start.2) | collective-permute-done | bytes 1572896 | tf_op jit(solution)/shard_map/ppermute | solution.py:31
  201.8 29.0 %broadcast_multiply_fusion = (f32[4,32,48,128]{3,2,1,0:T(8,128)S(1)}, f32[4,32,48,128]{3,2,1,0:T(8,128)}) fusion(f32[4,32,48,128]{3,2,1,0:T(8,128)S(1)} %copy-done, f32[2,32,48,128]{3,2,1,0:T(8,128)} %bitcast.108, f32[2,32,48,128]{3,2,1,0:T(8,128)} %add.258, f32[4,32,48]{2,1,0:T(8,128)} %param.7, f32[4,32,4,128]{3,2,1,0:T(4,128)} %get-tuple-element.95, ...), kind=kLoop, calls=%fused_computation.99 | loop fusion | flops 47972352 | bytes 88104960 | tf_op jit(solution)/shard_map/div | solution.py:102
  254.1 47.8 %collective-permute-done.3 = f32[4,32,48,128]{3,2,1,0:T(8,128)S(1)} collective-permute-done((f32[4,32,48,128]{3,2,1,0:T(8,128)S(1)}, f32[4,32,48,128]{3,2,1,0:T(8,128)S(1)}, u32[]{:S(2)}, u32[]{:S(2)}) %collective-permute-start.3) | collective-permute-done | bytes 3145760 | tf_op jit(solution)/shard_map/ppermute | solution.py:23
  305.7 8.0 convolution_bitcast_fusion
  324.4 77.6 %collective-permute-done.5 = f32[2,32,48,128]{3,2,1,0:T(8,128)S(1)} collective-permute-done((f32[2,32,48,128]{3,2,1,0:T(8,128)S(1)}, f32[2,32,48,128]{3,2,1,0:T(8,128)S(1)}, u32[]{:S(2)}, u32[]{:S(2)}) %collective-permute-start.5) | collective-permute-done | bytes 1572896 | tf_op jit(solution)/shard_map/ppermute | solution.py:31
  405.0 25.2 %multiply_subtract_fusion = f32[4,32,48,128]{3,2,1,0:T(8,128)} fusion(f32[4,32,48,128]{3,2,1,0:T(8,128)S(1)} %copy-done, f32[4,32,48,128]{3,2,1,0:T(8,128)S(1)} %copy-done.2, f32[2,32,48,128]{3,2,1,0:T(8,128)S(1)} %bitcast.109, f32[2,32,48,128]{3,2,1,0:T(8,128)} %add.285, f32[4,32,4,128]{3,2,1,0:T(4,128)} %get-tuple-element.61, ...), kind=kLoop, calls=%fused_computation.97 | loop fusion | flops 53477376 | bytes 72376320 | tf_op jit(solution)/shard_map/sub | solution.py:104
  430.3 85.4 %all-gather.2.cloned.1.call-done = f32[6144,512]{1,0:T(8,128)} async-done(((f32[6144,128]{1,0:T(8,128)}), f32[6144,512]{1,0:T(8,128)}) %all-gather.2.cloned.1.call-update) | async-done | bytes 12582928 | tf_op jit(solution)/shard_map/all_gather | solution.py:110
  515.6 26.2 %fusion.155 = f32[512,512]{0,1:T(8,128)} fusion(f32[6144,512]{1,0:T(8,128)} %all-gather.2.cloned.1.call-done), kind=kOutput, calls=%fused_computation.243 | convolution fusion | flops 19327352832 | bytes 13631488 | tf_op jit(solution)/shard_map/dot_general | solution.py:111
  543.8 307.9 %all-reduce.3.cloned.1.call-done = f32[512,512]{0,1:T(8,128)} async-done(((f32[512,512]{0,1:T(8,128)}), f32[512,512]{0,1:T(8,128)}) %all-reduce.3.cloned.1.call-update) | async-done | bytes 1048592 | tf_op jit(solution)/shard_map/psum | solution.py:112
  853.7 11.7 %cholesky.104 = f32[128,128]{1,0:T(8,128)S(1)} custom-call(f32[128,128]{1,0:T(8,128)S(1)} %cholesky.266), custom_call_target="Cholesky" | custom-call | tf_op jit(solution)/shard_map/jit(cholesky)/cholesky | solution.py:113
  865.6 9.8 custom-call.31
  877.1 11.7 %cholesky.217 = f32[128,128]{1,0:T(8,128)S(1)} custom-call(f32[128,128]{1,0:T(8,128)S(1)} %cholesky.270), custom_call_target="Cholesky" | custom-call | tf_op jit(solution)/shard_map/jit(cholesky)/cholesky | solution.py:113
  888.9 10.0 custom-call.32
  900.5 11.7 %cholesky.238 = f32[128,128]{1,0:T(8,128)S(1)} custom-call(f32[128,128]{1,0:T(8,128)S(1)} %cholesky.275), custom_call_target="Cholesky" | custom-call | tf_op jit(solution)/shard_map/jit(cholesky)/cholesky | solution.py:113
  912.9 9.8 custom-call.33
  924.1 11.9 %cholesky.255 = f32[128,128]{1,0:T(8,128)S(1)} custom-call(f32[128,128]{1,0:T(8,128)S(1)} %convolution_subtract_fusion.5), custom_call_target="Cholesky" | custom-call | tf_op jit(solution)/shard_map/jit(cholesky)/cholesky | solution.py:113
  940.0 10.1 while.1
  950.1 40.1 %custom-call.34 = f32[4,128,128]{1,2,0:T(8,128)S(1)} custom-call(f32[4,128,128]{2,1,0:T(8,128)} %get-tuple-element.9), custom_call_target="InvertDiagBlocksLowerTriangular" | custom-call | tf_op jit(solution)/shard_map/jit(_solve_triangular)/triangular_solve | solution.py:114
  994.1 13.8 %fusion.81 = f32[6144,128]{1,0:T(8,128)} fusion(f32[6144,512]{1,0:T(8,128)} %all-gather.2.cloned.1.call-done, s32[]{:T(128)S(6)} %select_n.8, f32[128,512]{1,0:T(8,128)S(1)} %fusion.84, f32[128,512]{1,0:T(8,128)S(1)} %fusion.96, f32[128,512]{1,0:T(8,128)S(1)} %fusion.94, f32[128,512]{1,0:T(8,128)S(1)} %fusion.93), kind=kOutput, calls=%fused_computation.138 | convolution fusion | flops 4832034816 | bytes 16777220 | tf_op jit(solution)/shard_map/dot_general | solution.py:116
  (135 shorter events, 115.3 us)
Async XLA Ops:
  7.2 13.9 %copy-start = (f32[4,32,48,128]{3,2,1,0:T(8,128)S(1)}, f32[4,32,48,128]{3,2,1,0:T(8,128)}, u32[]{:S(2)}) copy-start(f32[4,32,48,128]{3,2,1,0:T(8,128)} %param.6) | copy-start | bytes 9437188
  7.2 508.5 %all-gather.2.cloned.1.call-start = ((), (), s32[]{:S(2)}) async-start(), calls=%async_computation | async-start | bytes 15728640 | tf_op jit(solution)/shard_map/all_gather | solution.py:110
  7.2 76.8 %collective-permute-start.1 = (f32[4,32,48,128]{3,2,1,0:T(8,128)}, f32[4,32,48,128]{3,2,1,0:T(8,128)}, u32[]{:S(2)}, u32[]{:S(2)}) collective-permute-start(f32[4,32,48,128]{3,2,1,0:T(8,128)} %param.6), channel_id=1, source_target_pairs={{0,1},{1,2},{2,3},{3,4},{4,5},{5,6},{6,7},{7,8},{8,9},{9,10},{10,1... | collective-permute-start | bytes 9437192 | tf_op jit(solution)/shard_map/ppermute | solution.py:22
  8.9 137.1 %collective-permute-start = (f32[4,32,48,128]{3,2,1,0:T(8,128)}, f32[4,32,48,128]{3,2,1,0:T(8,128)}, u32[]{:S(2)}, u32[]{:S(2)}) collective-permute-start(f32[4,32,48,128]{3,2,1,0:T(8,128)} %param.6), channel_id=1, source_target_pairs={{1,0},{2,1},{3,2},{4,3},{5,4},{6,5},{7,6},{8,7},{9,8},{10,9},{11,1... | collective-permute-start | bytes 9437192 | tf_op jit(solution)/shard_map/ppermute | solution.py:23
  14.9 11.7 %copy-start.12 = (f32[8,4,4]{0,2,1:T(4,128)S(1)}, f32[8,4,4]{0,2,1:T(4,128)}, u32[]{:S(2)}) copy-start(f32[8,4,4]{0,2,1:T(4,128)} %param.9) | copy-start | bytes 1540
  14.9 11.8 %copy-start.13 = (s32[8]{0:T(128)S(1)}, s32[8]{0:T(128)}, u32[]{:S(2)}) copy-start(s32[8]{0:T(128)} %param.10) | copy-start | bytes 100
  30.4 121.3 %copy-start.3 = (f32[8,4,6,1536]{3,2,1,0:T(8,128)}, f32[8,4,6,1536]{3,2,1,0:T(8,128)S(1)}, u32[]{:S(2)}) copy-start(f32[8,4,6,1536]{3,2,1,0:T(8,128)S(1)} %convolution_bitcast_fusion.2) | copy-start | bytes 3538948
  86.7 64.9 %copy-start.1 = (f32[8,32,48,128]{3,2,1,0:T(8,128)}, f32[8,32,48,128]{3,2,1,0:T(8,128)S(1)}, u32[]{:S(2)}) copy-start(f32[8,32,48,128]{3,2,1,0:T(8,128)S(1)} %get-tuple-element.80) | copy-start | bytes 18874372
  159.5 2.9 copy-start.11
  160.9 39.5 %collective-permute-start.2 = (f32[2,32,48,128]{3,2,1,0:T(8,128)S(1)}, f32[2,32,48,128]{3,2,1,0:T(8,128)S(1)}, u32[]{:S(2)}, u32[]{:S(2)}) collective-permute-start(f32[2,32,48,128]{3,2,1,0:T(8,128)S(1)} %bitcast.112), channel_id=1, source_target_pairs={{0,1},{1,2},{2,3},{3,4},{4,5},{5,6},{6,7},{7,8},{8,9},{9,10},{10,1... | collective-permute-start | bytes 4718600 | tf_op jit(solution)/shard_map/ppermute | solution.py:31
  173.1 28.7 %copy-start.10 = (f32[4,1,48,128]{3,2,1,0:T(8,128)S(1)}, f32[4,1,48,128]{3,2,1,0:T(8,128)}, u32[]{:S(2)}) copy-start(f32[4,1,48,128]{3,2,1,0:T(8,128)} %get-tuple-element.64) | copy-start | bytes 294916
  230.8 71.1 %collective-permute-start.3 = (f32[4,32,48,128]{3,2,1,0:T(8,128)S(1)}, f32[4,32,48,128]{3,2,1,0:T(8,128)S(1)}, u32[]{:S(2)}, u32[]{:S(2)}) collective-permute-start(f32[4,32,48,128]{3,2,1,0:T(8,128)S(1)} %get-tuple-element.22), channel_id=1, source_target_pairs={{1,0},{2,1},{3,2},{4,3},{5,4},{6,5},{7,6},{8,7},{9,8},{10,9},{11,1... | collective-permute-start | bytes 9437192 | tf_op jit(solution)/shard_map/ppermute | solution.py:23
  234.3 169.0 %collective-permute-start.4 = (f32[4,32,48,128]{3,2,1,0:T(8,128)S(1)}, f32[4,32,48,128]{3,2,1,0:T(8,128)S(1)}, u32[]{:S(2)}, u32[]{:S(2)}) collective-permute-start(f32[4,32,48,128]{3,2,1,0:T(8,128)S(1)} %get-tuple-element.22), channel_id=1, source_target_pairs={{0,1},{1,2},{2,3},{3,4},{4,5},{5,6},{6,7},{7,8},{8,9},{9,10},{10,1... | collective-permute-start | bytes 9437192 | tf_op jit(solution)/shard_map/ppermute | solution.py:22
  254.1 48.4 %copy-start.4 = (f32[8,4,6,1536]{3,2,1,0:T(8,128)S(1)}, f32[8,4,6,1536]{3,2,1,0:T(8,128)}, u32[]{:S(2)}) copy-start(f32[8,4,6,1536]{3,2,1,0:T(8,128)} %copy-done.3) | copy-start | bytes 3538948
  314.0 88.0 %collective-permute-start.5 = (f32[2,32,48,128]{3,2,1,0:T(8,128)S(1)}, f32[2,32,48,128]{3,2,1,0:T(8,128)S(1)}, u32[]{:S(2)}, u32[]{:S(2)}) collective-permute-start(f32[2,32,48,128]{3,2,1,0:T(8,128)S(1)} %bitcast.111), channel_id=1, source_target_pairs={{0,1},{1,2},{2,3},{3,4},{4,5},{5,6},{6,7},{7,8},{8,9},{9,10},{10,1... | collective-permute-start | bytes 4718600 | tf_op jit(solution)/shard_map/ppermute | solution.py:31
  324.4 80.6 %copy-start.2 = (f32[4,32,48,128]{3,2,1,0:T(8,128)S(1)}, f32[4,32,48,128]{3,2,1,0:T(8,128)}, u32[]{:S(2)}) copy-start(f32[4,32,48,128]{3,2,1,0:T(8,128)} %get-tuple-element.23) | copy-start | bytes 9437188
  403.3 1.6 copy-start.8
  430.2 421.5 %all-reduce.3.cloned.1.call-start = ((), (), s32[]{:S(2)}) async-start(), calls=%async_computation.1 | async-start | bytes 2097152 | tf_op jit(solution)/shard_map/psum | solution.py:112
  851.7 1.8 copy-start.6
  853.4 45.7 %copy-start.5 = (f32[512,512]{1,0:T(8,128)}, f32[512,512]{1,0:T(8,128)S(1)}, u32[]{:S(2)}) copy-start(f32[512,512]{1,0:T(8,128)S(1)} %copy.20) | copy-start | bytes 3145732
  853.7 22.0 %copy-start.9 = (f32[512,512]{1,0:T(8,128)}, f32[512,512]{1,0:T(8,128)S(1)}, u32[]{:S(2)}) copy-start(f32[512,512]{1,0:T(8,128)S(1)} %fusion.64) | copy-start | bytes 3145732
  875.8 115.6 %copy-start.7 = (f32[512,512]{1,0:T(8,128)S(1)}, f32[512,512]{1,0:T(8,128)}, u32[]{:S(2)}) copy-start(f32[512,512]{1,0:T(8,128)} %fusion.77) | copy-start | bytes 3145732
Sparse Core Ops, SparseCore 0:
  430.3 85.2 all-gather.1
  542.0 309.6 all-reduce.2
where the time goes:
time: 1020 us
  waiting for transfers between devices  646 us (63%)
  other arithmetic  181 us (18%)
  local copies, waits for them, and re-layouts  85.5 us (8%)
  matrix products  72.9 us (7%)
  between operations  17.4 us (2%)
  starting transfers between devices  11.6 us (1%)
    psum x1, waiting for transfers between devices, shards(): gram = lax.psum(partial_gram, 'dom') * (1.0 / total_cells)  308 us
    ppermute x2, waiting for transfers between devices, with_halo(): after = lax.ppermute(first, axis, down)  107 us
    ppermute x2, waiting for transfers between devices, passed_along(): return lax.ppermute(value, axis, pairs)  105 us
    all_gather x1, waiting for transfers between devices, shards(): panels = lax.all_gather(flat, 'band', axis=1, tiled=True)  85.4 us
    another operation x14, other arithmetic, shards(): lower = jnp.linalg.cholesky(gram)  78.8 us
    ppermute x2, waiting for transfers between devices, with_halo(): before = lax.ppermute(last, axis, up)  41 us
    another operation x3, other arithmetic, shards(): inverse = jax.scipy.linalg.solve_triangular(lower, identity, lower=True)  40.3 us
    slice x16, local copies, waits for them, and re-layouts, laplacian(): jnp.roll(orbital_field, offset, 2) + jnp.roll(orbital_field, -offset, 2)  32.4 us
  transfers between devices with their start and end apart: 8, of which 7 were waited for; matrix products, arithmetic and copies ran while one was open for 9% of the time, Pallas kernels for 0%

commit v1 on v0

--- a/solution.py
+++ b/solution.py
@@ -107,7 +107,10 @@
     total_cells = cells * lax.axis_size("dom")
     flat = second.reshape(cells, local_orbs)
     identity = jnp.eye(NORB, dtype=jnp.float32)
-    panels = lax.all_gather(flat, "band", axis=1, tiled=True)
+    size = lax.axis_size("band")
+    pieces = jnp.stack([flat for _ in range(size)])
+    pieces = lax.all_to_all(pieces, "band", split_axis=0, concat_axis=0)
+    panels = jnp.concatenate(pieces, axis=1)
     partial_gram = jnp.dot(panels.T, panels, precision=HIGH, preferred_element_type=jnp.float32)
     gram = lax.psum(partial_gram, "dom") * (1.0 / total_cells)
     lower = jnp.linalg.cholesky(gram)

time: 1020 us -> 1090 us (1.069)
  blocking collectives: 0 us -> 144 us
  waiting for transfers between devices: 646 us -> 525 us
  local copies, waits for them, and re-layouts: 85.5 us -> 133 us
    all_to_all x0 -> x1, blocking collectives: none -> 144 us  [shards(): pieces = lax.all_to_all(pieces, 'band', split_axis=0, concat_axis=0)]
    all_gather x1 -> x0, waiting for transfers between devices: 85.4 us -> none  [shards(): panels = lax.all_gather(flat, 'band', axis=1, tiled=True)]
    psum x1, waiting for transfers between devices: 308 us -> 272 us  [shards(): gram = lax.psum(partial_gram, 'dom') * (1.0 / total_cells)]
    reshape x0 -> x1, local copies, waits for them, and re-layouts: none -> 16.4 us  [shards(): panels = jnp.concatenate(pieces, axis=1)]
    dot_general x0 -> x1, local copies, waits for them, and re-layouts: none -> 15.3 us  [shards(): jnp.dot(panels, own_rows.T, precision=HIGH, preferred_element_type=jnp.fl...]
    all_to_all x0 -> x1, local copies, waits for them, and re-layouts: none -> 12.6 us  [shards(): pieces = lax.all_to_all(pieces, 'band', split_axis=0, concat_axis=0)]
  transfers between devices with their start and end apart: 8 -> 7, of which waited for: 7 -> 6; matrix products, arithmetic and copies ran while one was open for 9% -> 11% of each run, Pallas kernels for 0% -> 0%
where the time goes in v1:
time: 1090 us; the launch traced here: 1080 us
  waiting for transfers between devices  525 us (48%)
  other arithmetic  181 us (17%)
  blocking collectives  144 us (13%)
  local copies, waits for them, and re-layouts  133 us (12%)
  matrix products  71.1 us (7%)
  between operations  17.3 us (2%)
  starting transfers between devices  11.5 us (1%)
    psum x1, waiting for transfers between devices, shards(): gram = lax.psum(partial_gram, 'dom') * (1.0 / total_cells)  272 us
    all_to_all x1, blocking collectives, shards(): pieces = lax.all_to_all(pieces, 'band', split_axis=0, concat_axis=0)  144 us
    ppermute x2, waiting for transfers between devices, with_halo(): after = lax.ppermute(first, axis, down)  107 us
    ppermute x2, waiting for transfers between devices, passed_along(): return lax.ppermute(value, axis, pairs)  105 us
    another operation x14, other arithmetic, shards(): lower = jnp.linalg.cholesky(gram)  79 us
    ppermute x2, waiting for transfers between devices, with_halo(): before = lax.ppermute(last, axis, up)  41.1 us
    another operation x3, other arithmetic, shards(): inverse = jax.scipy.linalg.solve_triangular(lower, identity, lower=True)  40.3 us
    slice x16, local copies, waits for them, and re-layouts, laplacian(): jnp.roll(orbital_field, offset, 2) + jnp.roll(orbital_field, -offset, 2)  32.5 us
  transfers between devices with their start and end apart: 7, of which 6 were waited for; matrix products, arithmetic and copies ran while one was open for 11% of the time, Pallas kernels for 0%

profile of v1, /device:TPU:0, one launch (start us, length us, event | category | flops | bytes accessed | tf_op | source)
XLA Modules:
  0.0 1083.4 jit_solution(12465063279801248917)
XLA Ops:
  43.0 41.1 %collective-permute-done.1 = f32[4,32,48,128]{3,2,1,0:T(8,128)} collective-permute-done((f32[4,32,48,128]{3,2,1,0:T(8,128)}, f32[4,32,48,128]{3,2,1,0:T(8,128)}, u32[]{:S(2)}, u32[]{:S(2)}) %collective-permute-start.1) | collective-permute-done | bytes 3145760 | tf_op jit(solution)/shard_map/ppermute | solution.py:22
  86.7 59.3 %collective-permute-done = f32[4,32,48,128]{3,2,1,0:T(8,128)} collective-permute-done((f32[4,32,48,128]{3,2,1,0:T(8,128)}, f32[4,32,48,128]{3,2,1,0:T(8,128)}, u32[]{:S(2)}, u32[]{:S(2)}) %collective-permute-start) | collective-permute-done | bytes 3145760 | tf_op jit(solution)/shard_map/ppermute | solution.py:23
  173.1 27.3 %collective-permute-done.2 = f32[2,32,48,128]{3,2,1,0:T(8,128)S(1)} collective-permute-done((f32[2,32,48,128]{3,2,1,0:T(8,128)S(1)}, f32[2,32,48,128]{3,2,1,0:T(8,128)S(1)}, u32[]{:S(2)}, u32[]{:S(2)}) %collective-permute-start.2) | collective-permute-done | bytes 1572896 | tf_op jit(solution)/shard_map/ppermute | solution.py:31
  201.8 28.7 %broadcast_multiply_fusion = (f32[4,32,48,128]{3,2,1,0:T(8,128)S(1)}, f32[4,32,48,128]{3,2,1,0:T(8,128)}) fusion(f32[4,32,48,128]{3,2,1,0:T(8,128)S(1)} %copy-done, f32[2,32,48,128]{3,2,1,0:T(8,128)} %bitcast.118, f32[2,32,48,128]{3,2,1,0:T(8,128)} %add.258, f32[4,32,48]{2,1,0:T(8,128)} %param.7, f32[4,32,4,128]{3,2,1,0:T(4,128)} %get-tuple-element.99, ...), kind=kLoop, calls=%fused_computation.99 | loop fusion | flops 47972352 | bytes 88104960 | tf_op jit(solution)/shard_map/div | solution.py:102
  253.5 48.1 %collective-permute-done.3 = f32[4,32,48,128]{3,2,1,0:T(8,128)S(1)} collective-permute-done((f32[4,32,48,128]{3,2,1,0:T(8,128)S(1)}, f32[4,32,48,128]{3,2,1,0:T(8,128)S(1)}, u32[]{:S(2)}, u32[]{:S(2)}) %collective-permute-start.3) | collective-permute-done | bytes 3145760 | tf_op jit(solution)/shard_map/ppermute | solution.py:23
  305.4 7.9 convolution_bitcast_fusion
  324.1 77.6 %collective-permute-done.5 = f32[2,32,48,128]{3,2,1,0:T(8,128)S(1)} collective-permute-done((f32[2,32,48,128]{3,2,1,0:T(8,128)S(1)}, f32[2,32,48,128]{3,2,1,0:T(8,128)S(1)}, u32[]{:S(2)}, u32[]{:S(2)}) %collective-permute-start.5) | collective-permute-done | bytes 1572896 | tf_op jit(solution)/shard_map/ppermute | solution.py:31
  404.7 25.3 %multiply_subtract_fusion = f32[4,32,48,128]{3,2,1,0:T(8,128)} fusion(f32[4,32,48,128]{3,2,1,0:T(8,128)S(1)} %copy-done, f32[4,32,48,128]{3,2,1,0:T(8,128)S(1)} %copy-done.2, f32[2,32,48,128]{3,2,1,0:T(8,128)S(1)} %bitcast.119, f32[2,32,48,128]{3,2,1,0:T(8,128)} %add.285, f32[4,32,4,128]{3,2,1,0:T(4,128)} %get-tuple-element.65, ...), kind=kLoop, calls=%fused_computation.97 | loop fusion | flops 53477376 | bytes 72376320 | tf_op jit(solution)/shard_map/sub | solution.py:104
  432.6 143.8 %all_to_all.5 = f32[4,6144,128]{2,1,0:T(8,128)} all-to-all(f32[4,6144,128]{2,1,0:T(8,128)S(1)} %stack.3), channel_id=1, replica_groups=mesh['band'=4,'dom'=32] {'band'}, dimensions={0} | all-to-all | bytes 25165824 | tf_op jit(solution)/shard_map/all_to_all | solution.py:112
  576.4 12.6 %copy.52 = f32[4,6144,128]{1,2,0:T(8,128)} copy(f32[4,6144,128]{2,1,0:T(8,128)} %all_to_all.5) | data formatting | bytes 25165824 | tf_op jit(solution)/shard_map/all_to_all | solution.py:112
  589.1 24.4 %fusion.156 = f32[512,512]{0,1:T(8,128)} fusion(f32[6144,512]{0,1:T(8,128)} %bitcast.111), kind=kOutput, calls=%fused_computation.244 | convolution fusion | flops 19327352832 | bytes 13631488 | tf_op jit(solution)/shard_map/dot_general | solution.py:114
  615.4 16.4 %copy.53 = f32[6144,4,128]{2,1,0:T(4,128)} copy(f32[6144,4,128]{2,0,1:T(8,128)} %bitcast.112) | data formatting | bytes 25165824 | tf_op jit(solution)/shard_map/reshape | solution.py:113
  631.8 15.3 %dot_general.36 = f32[4,32,48,512]{3,2,1,0:T(8,128)} reshape(f32[6144,4,128]{2,1,0:T(4,128)} %copy.53) | data formatting | bytes 25165824 | tf_op jit(solution)/shard_map/dot_general | solution.py:119
  647.2 271.8 %all-reduce.3.cloned.1.call-done = f32[512,512]{0,1:T(8,128)} async-done(((f32[512,512]{0,1:T(8,128)}), f32[512,512]{0,1:T(8,128)}) %all-reduce.3.cloned.1.call-update) | async-done | bytes 1048592 | tf_op jit(solution)/shard_map/psum | solution.py:115
  921.0 11.7 %cholesky.104 = f32[128,128]{1,0:T(8,128)S(1)} custom-call(f32[128,128]{1,0:T(8,128)S(1)} %cholesky.266), custom_call_target="Cholesky" | custom-call | tf_op jit(solution)/shard_map/jit(cholesky)/cholesky | solution.py:116
  932.9 9.8 custom-call.31
  944.4 11.7 %cholesky.217 = f32[128,128]{1,0:T(8,128)S(1)} custom-call(f32[128,128]{1,0:T(8,128)S(1)} %cholesky.270), custom_call_target="Cholesky" | custom-call | tf_op jit(solution)/shard_map/jit(cholesky)/cholesky | solution.py:116
  956.2 10.2 custom-call.32
  967.9 11.7 %cholesky.238 = f32[128,128]{1,0:T(8,128)S(1)} custom-call(f32[128,128]{1,0:T(8,128)S(1)} %cholesky.275), custom_call_target="Cholesky" | custom-call | tf_op jit(solution)/shard_map/jit(cholesky)/cholesky | solution.py:116
  980.4 9.8 custom-call.33
  991.7 11.7 %cholesky.255 = f32[128,128]{1,0:T(8,128)S(1)} custom-call(f32[128,128]{1,0:T(8,128)S(1)} %convolution_subtract_fusion.5), custom_call_target="Cholesky" | custom-call | tf_op jit(solution)/shard_map/jit(cholesky)/cholesky | solution.py:116
  1007.6 10.9 %while.1 = (s32[]{:T(128)}, f32[512,512]{1,0:T(8,128)S(1)}, s32[4,2]{0,1:T(2,128)S(1)}, f32[4,128,128]{2,1,0:T(8,128)}, s32[]{:T(128)}) while((s32[]{:T(128)}, f32[512,512]{1,0:T(8,128)S(1)}, s32[4,2]{0,1:T(2,128)S(1)}, f32[4,128,128]{2,1,0:T(8,128)}, s32[]{:T(128)}) %tuple.73), condition=%wide.while_cond, body=%wide.while_body.sunk | while | flops 2 | bytes 132705 | solution.py:117
  1018.6 40.1 %custom-call.34 = f32[4,128,128]{1,2,0:T(8,128)S(1)} custom-call(f32[4,128,128]{2,1,0:T(8,128)} %get-tuple-element.9), custom_call_target="InvertDiagBlocksLowerTriangular" | custom-call | tf_op jit(solution)/shard_map/jit(_solve_triangular)/triangular_solve | solution.py:117
  1062.5 13.8 %fusion.82 = f32[4,32,48,128]{3,2,1,0:T(8,128)} fusion(f32[4,32,48,512]{3,2,1,0:T(8,128)} %dot_general.36, s32[]{:T(128)S(6)} %select_n.8, f32[128,512]{1,0:T(8,128)S(1)} %fusion.85, f32[128,512]{1,0:T(8,128)S(1)} %fusion.97, f32[128,512]{1,0:T(8,128)S(1)} %fusion.95, f32[128,512]{1,0:T(8,128)S(1)} %fusion.94), kind=kOutput, calls=%fused_computation.139 | convolution fusion | flops 4832034816 | bytes 16777220 | tf_op jit(solution)/shard_map/dot_general | solution.py:119
  (137 shorter events, 135.9 us)
Async XLA Ops:
  7.2 13.9 %copy-start = (f32[4,32,48,128]{3,2,1,0:T(8,128)S(1)}, f32[4,32,48,128]{3,2,1,0:T(8,128)}, u32[]{:S(2)}) copy-start(f32[4,32,48,128]{3,2,1,0:T(8,128)} %param.6) | copy-start | bytes 9437188
  7.2 911.8 %all-reduce.3.cloned.1.call-start = ((), (), s32[]{:S(2)}) async-start(), calls=%async_computation.1 | async-start | bytes 2097152 | tf_op jit(solution)/shard_map/psum | solution.py:115
  7.2 76.8 %collective-permute-start.1 = (f32[4,32,48,128]{3,2,1,0:T(8,128)}, f32[4,32,48,128]{3,2,1,0:T(8,128)}, u32[]{:S(2)}, u32[]{:S(2)}) collective-permute-start(f32[4,32,48,128]{3,2,1,0:T(8,128)} %param.6), channel_id=1, source_target_pairs={{0,1},{1,2},{2,3},{3,4},{4,5},{5,6},{6,7},{7,8},{8,9},{9,10},{10,1... | collective-permute-start | bytes 9437192 | tf_op jit(solution)/shard_map/ppermute | solution.py:22
  8.9 137.1 %collective-permute-start = (f32[4,32,48,128]{3,2,1,0:T(8,128)}, f32[4,32,48,128]{3,2,1,0:T(8,128)}, u32[]{:S(2)}, u32[]{:S(2)}) collective-permute-start(f32[4,32,48,128]{3,2,1,0:T(8,128)} %param.6), channel_id=1, source_target_pairs={{1,0},{2,1},{3,2},{4,3},{5,4},{6,5},{7,6},{8,7},{9,8},{10,9},{11,1... | collective-permute-start | bytes 9437192 | tf_op jit(solution)/shard_map/ppermute | solution.py:23
  14.9 11.7 %copy-start.12 = (f32[8,4,4]{0,2,1:T(4,128)S(1)}, f32[8,4,4]{0,2,1:T(4,128)}, u32[]{:S(2)}) copy-start(f32[8,4,4]{0,2,1:T(4,128)} %param.9) | copy-start | bytes 1540
  14.9 11.8 %copy-start.13 = (s32[8]{0:T(128)S(1)}, s32[8]{0:T(128)}, u32[]{:S(2)}) copy-start(s32[8]{0:T(128)} %param.10) | copy-start | bytes 100
  30.5 121.3 %copy-start.3 = (f32[8,4,6,1536]{3,2,1,0:T(8,128)}, f32[8,4,6,1536]{3,2,1,0:T(8,128)S(1)}, u32[]{:S(2)}) copy-start(f32[8,4,6,1536]{3,2,1,0:T(8,128)S(1)} %convolution_bitcast_fusion.2) | copy-start | bytes 3538948
  86.7 61.4 %copy-start.1 = (f32[8,32,48,128]{3,2,1,0:T(8,128)}, f32[8,32,48,128]{3,2,1,0:T(8,128)S(1)}, u32[]{:S(2)}) copy-start(f32[8,32,48,128]{3,2,1,0:T(8,128)S(1)} %get-tuple-element.84) | copy-start | bytes 18874372
  159.5 2.9 copy-start.11
  160.9 39.5 %collective-permute-start.2 = (f32[2,32,48,128]{3,2,1,0:T(8,128)S(1)}, f32[2,32,48,128]{3,2,1,0:T(8,128)S(1)}, u32[]{:S(2)}, u32[]{:S(2)}) collective-permute-start(f32[2,32,48,128]{3,2,1,0:T(8,128)S(1)} %bitcast.121), channel_id=1, source_target_pairs={{0,1},{1,2},{2,3},{3,4},{4,5},{5,6},{6,7},{7,8},{8,9},{9,10},{10,1... | collective-permute-start | bytes 4718600 | tf_op jit(solution)/shard_map/ppermute | solution.py:31
  173.1 28.7 %copy-start.10 = (f32[4,1,48,128]{3,2,1,0:T(8,128)S(1)}, f32[4,1,48,128]{3,2,1,0:T(8,128)}, u32[]{:S(2)}) copy-start(f32[4,1,48,128]{3,2,1,0:T(8,128)} %get-tuple-element.68) | copy-start | bytes 294916
  230.5 71.1 %collective-permute-start.3 = (f32[4,32,48,128]{3,2,1,0:T(8,128)S(1)}, f32[4,32,48,128]{3,2,1,0:T(8,128)S(1)}, u32[]{:S(2)}, u32[]{:S(2)}) collective-permute-start(f32[4,32,48,128]{3,2,1,0:T(8,128)S(1)} %get-tuple-element.26), channel_id=1, source_target_pairs={{1,0},{2,1},{3,2},{4,3},{5,4},{6,5},{7,6},{8,7},{9,8},{10,9},{11,1... | collective-permute-start | bytes 9437192 | tf_op jit(solution)/shard_map/ppermute | solution.py:23
  234.0 169.0 %collective-permute-start.4 = (f32[4,32,48,128]{3,2,1,0:T(8,128)S(1)}, f32[4,32,48,128]{3,2,1,0:T(8,128)S(1)}, u32[]{:S(2)}, u32[]{:S(2)}) collective-permute-start(f32[4,32,48,128]{3,2,1,0:T(8,128)S(1)} %get-tuple-element.26), channel_id=1, source_target_pairs={{0,1},{1,2},{2,3},{3,4},{4,5},{5,6},{6,7},{7,8},{8,9},{9,10},{10,1... | collective-permute-start | bytes 9437192 | tf_op jit(solution)/shard_map/ppermute | solution.py:22
  253.5 48.6 %copy-start.4 = (f32[8,4,6,1536]{3,2,1,0:T(8,128)S(1)}, f32[8,4,6,1536]{3,2,1,0:T(8,128)}, u32[]{:S(2)}) copy-start(f32[8,4,6,1536]{3,2,1,0:T(8,128)} %copy-done.3) | copy-start | bytes 3538948
  313.7 88.0 %collective-permute-start.5 = (f32[2,32,48,128]{3,2,1,0:T(8,128)S(1)}, f32[2,32,48,128]{3,2,1,0:T(8,128)S(1)}, u32[]{:S(2)}, u32[]{:S(2)}) collective-permute-start(f32[2,32,48,128]{3,2,1,0:T(8,128)S(1)} %bitcast.120), channel_id=1, source_target_pairs={{0,1},{1,2},{2,3},{3,4},{4,5},{5,6},{6,7},{7,8},{8,9},{9,10},{10,1... | collective-permute-start | bytes 4718600 | tf_op jit(solution)/shard_map/ppermute | solution.py:31
  324.1 80.6 %copy-start.2 = (f32[4,32,48,128]{3,2,1,0:T(8,128)S(1)}, f32[4,32,48,128]{3,2,1,0:T(8,128)}, u32[]{:S(2)}) copy-start(f32[4,32,48,128]{3,2,1,0:T(8,128)} %get-tuple-element.27) | copy-start | bytes 9437188
  403.0 1.6 copy-start.8
  919.0 1.8 copy-start.6
  920.7 45.9 %copy-start.5 = (f32[512,512]{1,0:T(8,128)}, f32[512,512]{1,0:T(8,128)S(1)}, u32[]{:S(2)}) copy-start(f32[512,512]{1,0:T(8,128)S(1)} %copy.55) | copy-start | bytes 3145732
  921.0 22.0 %copy-start.9 = (f32[512,512]{1,0:T(8,128)}, f32[512,512]{1,0:T(8,128)S(1)}, u32[]{:S(2)}) copy-start(f32[512,512]{1,0:T(8,128)S(1)} %fusion.64) | copy-start | bytes 3145732
  943.0 116.7 %copy-start.7 = (f32[512,512]{1,0:T(8,128)S(1)}, f32[512,512]{1,0:T(8,128)}, u32[]{:S(2)}) copy-start(f32[512,512]{1,0:T(8,128)} %fusion.77) | copy-start | bytes 3145732
Sparse Core Ops, SparseCore 0:
  613.6 305.3 all-reduce.2
